TPU v7x, 32 devices: a whole 2x2x4 slice. The times are simulated.
32 devices in a mesh: blk: 4 (over y, core), dp: 8 (over z, x).
Axes of the slice: x: 2, y: 2, z: 4, core: 2. Of those that a mesh axis runs over, the one named last changes fastest.
Arguments:
- tokens: bfloat16 [8, 1024, 384], P('dp', 'blk'), may hold values from -6 to 6
- lengths: int32 [8], P('dp'), may hold values from 512 to 1024, as said below
- query_weight: bfloat16 [384, 384], replicated, may hold values from -0.3125 to 0.3125
- query_bias: bfloat16 [384], replicated, may hold values from -1.5 to 1.5
- key_weight: bfloat16 [384, 384], replicated, may hold values from -0.3125 to 0.3125
- key_bias: bfloat16 [384], replicated, may hold values from -1.5 to 1.5
- value_weight: bfloat16 [384, 384], replicated, may hold values from -0.3125 to 0.3125
- value_bias: bfloat16 [384], replicated, may hold values from -1.5 to 1.5
- output_weight: bfloat16 [384, 384], replicated, may hold values from -2.5 to 2.5
- output_bias: bfloat16 [384], replicated, may hold values from -1.5 to 1.5
- first_gain: bfloat16 [384], replicated, may hold values from 0.5 to 1.5
- first_bias: bfloat16 [384], replicated, may hold values from -1.5 to 1.5
- inner_weight: bfloat16 [384, 1536], replicated, may hold values from -0.3125 to 0.3125
- inner_bias: bfloat16 [1536], replicated, may hold values from -1.5 to 1.5
- outer_weight: bfloat16 [1536, 384], replicated, may hold values from -0.15625 to 0.15625
- outer_bias: bfloat16 [384], replicated, may hold values from -1.5 to 1.5
- second_gain: bfloat16 [384], replicated, may hold values from 0.5 to 1.5
- second_bias: bfloat16 [384], replicated, may hold values from -1.5 to 1.5
- relative_table: bfloat16 [512, 384], replicated, may hold values from -6 to 6
- cotangent: bfloat16 [8, 1024, 384], P('dp', 'blk'), may hold values from -18 to 18
Outputs:
- layer_out: float32 [8, 1024, 384], P('dp', 'blk')
- grad_tokens: float32 [8, 1024, 384], P('dp', 'blk')
- grad_query_weight: float32 [384, 384], replicated
- grad_query_bias: float32 [384], replicated
- grad_key_weight: float32 [384, 384], replicated
- grad_key_bias: float32 [384], replicated
- grad_value_weight: float32 [384, 384], replicated
- grad_value_bias: float32 [384], replicated
- grad_output_weight: float32 [384, 384], replicated
- grad_output_bias: float32 [384], replicated
- grad_first_gain: float32 [384], replicated
- grad_first_bias: float32 [384], replicated
- grad_inner_weight: float32 [384, 1536], replicated
- grad_inner_bias: float32 [1536], replicated
- grad_outer_weight: float32 [1536, 384], replicated
- grad_outer_bias: float32 [384], replicated
- grad_second_gain: float32 [384], replicated
- grad_second_bias: float32 [384], replicated
- grad_relative_table: float32 [512, 384], replicated
Inputs may be any that keep to these rules, and one draw needn't show every extreme that they name: `lengths`: one sequence uses all 1024 positions and one uses 1024 // 2.
All inputs are finite; a program needn't handle non-finite values.
Results may differ from a plain program's by a relative error of at most 0.04.
Values may be sent and summed in bfloat16 or wider, within the bound.
No kernel may reach another device: no remote copies, remote signals or barrier semaphores. Data moves between devices by JAX's collectives and lax.ppermute only.
A program may use at most 320 MiB of HBM per device.

v0:
```python
from functools import partial
import math
import jax
import jax.numpy as jnp
from jax import lax
from jax.sharding import PartitionSpec as P

HEADS = 6


def layer_norm(values, gain_vec, bias_vec):
    center = values - jnp.mean(values, axis=-1, keepdims=True)
    spread = jnp.mean(center * center, axis=-1, keepdims=True)
    return center * lax.rsqrt(spread + 1e-07) * gain_vec + bias_vec


def skewed(source_table, row_count, col_count):
    table_width = row_count + col_count - 1
    leading = source_table.shape[:-2]
    padded = jnp.pad(source_table, [(0, 0)] * (source_table.ndim - 1) + [(0, 1)])
    flattened = padded.reshape(leading + (row_count * (table_width + 1),))
    flattened = flattened[..., row_count - 1 : row_count - 1 + row_count * table_width]
    return flattened.reshape(leading + (row_count, table_width))[..., :col_count]


def band_terms(query_table, key_table, band_shift):
    row_count = query_table.shape[2]
    col_count = key_table.shape[2]
    last_index = query_table.shape[3] - 1
    steps_along = jnp.arange(row_count + col_count - 1, dtype=jnp.int32)
    query_index = jnp.clip(band_shift + (row_count - 1) - steps_along, 0, last_index)
    to_position = skewed(jnp.take(query_table, query_index, axis=3), row_count, col_count)
    key_index = jnp.clip(band_shift - (col_count - 1) + steps_along, 0, last_index)
    from_position = skewed(jnp.take(key_table, key_index, axis=3), col_count, row_count)
    return to_position + jnp.swapaxes(from_position, 2, 3)


def split_einsum(formula, wide_values, narrow_values):
    upper_part = wide_values.astype(jnp.bfloat16)
    lower_part = (wide_values - upper_part.astype(jnp.float32)).astype(jnp.bfloat16)
    return jnp.einsum(
        formula, upper_part, narrow_values, preferred_element_type=jnp.float32
    ) + jnp.einsum(formula, lower_part, narrow_values, preferred_element_type=jnp.float32)


def project(values, weight, bias_vec):
    return jnp.dot(values, weight, preferred_element_type=jnp.float32) + bias_vec.astype(
        jnp.float32
    )


def weight_grad(left_rows, right_rows):
    return jnp.einsum("sbi,sbo->io", left_rows, right_rows, preferred_element_type=jnp.float32)


def bias_grad(grad_rows):
    return jnp.sum(grad_rows.astype(jnp.float32), axis=(0, 1))


def back_through(grad_rows, weight):
    return jnp.einsum("sbo,io->sbi", grad_rows, weight, preferred_element_type=jnp.float32)


def on_device(
    tokens,
    lengths,
    query_weight,
    query_bias,
    key_weight,
    key_bias,
    value_weight,
    value_bias,
    output_weight,
    output_bias,
    first_gain,
    first_bias,
    inner_weight,
    inner_bias,
    outer_weight,
    outer_bias,
    second_gain,
    second_bias,
    relative_table,
    cotangent,
):
    seq_count, row_count, model_width = tokens.shape
    head_dim = model_width // HEADS
    rel_count = relative_table.shape[0]
    span_half = rel_count // 2
    score_scale = 1.0 / math.sqrt(3.0 * head_dim)
    block_count = lax.axis_size("blk")
    block_index = lax.axis_index("blk")
    first_row = block_index * row_count
    query_rows = project(tokens, query_weight, query_bias).astype(jnp.bfloat16)
    key_rows = project(tokens, key_weight, key_bias).astype(jnp.bfloat16)
    value_rows = project(tokens, value_weight, value_bias).astype(jnp.bfloat16)
    rel_keys = (
        project(relative_table, key_weight, key_bias)
        .astype(jnp.bfloat16)
        .reshape(rel_count, HEADS, head_dim)
    )
    rel_queries = (
        project(relative_table, query_weight, query_bias)
        .astype(jnp.bfloat16)
        .reshape(rel_count, HEADS, head_dim)
    )
    query_heads = query_rows.reshape(seq_count, row_count, HEADS, head_dim)
    query_table = jnp.einsum(
        "sihd,rhd->shir", query_heads, rel_keys, preferred_element_type=jnp.float32
    )

    def block_scores(key_block, offset, with_pull):
        block_len = key_block.shape[1]
        key_heads = key_block.reshape(seq_count, block_len, HEADS, head_dim)
        content = jnp.einsum(
            "sihd,sjhd->shij", query_heads, key_heads, preferred_element_type=jnp.float32
        )
        key_table = jnp.einsum(
            "sjhd,rhd->shjr", key_heads, rel_queries, preferred_element_type=jnp.float32
        )
        band_shift = first_row - offset + span_half
        if with_pull:
            band_part, band_pull = jax.vjp(
                lambda left_table, right_table: band_terms(left_table, right_table, band_shift),
                query_table,
                key_table,
            )
        else:
            band_part = band_terms(query_table, key_table, band_shift)
            band_pull = None
        key_mask = (offset + jnp.arange(block_len, dtype=jnp.int32))[None, :] < lengths[:, None]
        key_mask = key_mask[:, None, None, :]
        scores = jnp.where(key_mask, (content + band_part) * score_scale, -1e30)
        return (scores, key_mask, key_heads, band_pull)

    block_ids = jnp.arange(block_count, dtype=jnp.int32)
    running_max = jnp.full((seq_count, HEADS, row_count), -1e30, jnp.float32)
    scores, key_mask, key_heads, unused_pull = block_scores(
        lax.all_gather(key_rows, "blk", axis=1, tiled=True), jnp.int32(0), False
    )
    next_max = jnp.maximum(running_max, jnp.max(scores, axis=-1))
    weights_now = jnp.where(key_mask, jnp.exp(scores - next_max[..., None]), 0.0)
    denominator = jnp.sum(weights_now, axis=-1)
    running_max, denominator = (next_max, denominator)
    log_total = running_max + jnp.log(denominator)
    scores, key_mask, key_heads, unused_pull = block_scores(
        lax.all_gather(key_rows, "blk", axis=1, tiled=True), jnp.int32(0), False
    )
    value_heads = lax.all_gather(value_rows, "blk", axis=1, tiled=True).reshape(key_heads.shape)
    chances = jnp.where(key_mask, jnp.exp(scores - log_total[..., None]), 0.0)
    weighted = jnp.einsum(
        "shij,sjhd->shid",
        chances.astype(jnp.bfloat16),
        value_heads,
        preferred_element_type=jnp.float32,
    )
    mixture = jnp.transpose(weighted, (0, 2, 1, 3)).reshape(seq_count, row_count, model_width)
    mixture_low = mixture.astype(jnp.bfloat16)
    branch_out = project(mixture_low, output_weight, output_bias)
    first_sum = tokens.astype(jnp.float32) + branch_out
    normed_f, first_pull = jax.vjp(
        layer_norm, first_sum, first_gain.astype(jnp.float32), first_bias.astype(jnp.float32)
    )
    normed = normed_f.astype(jnp.bfloat16)
    inner_pre = project(normed, inner_weight, inner_bias)
    active_f, gelu_pull = jax.vjp(partial(jax.nn.gelu, approximate=False), inner_pre)
    active = active_f.astype(jnp.bfloat16)
    outer_out = project(active, outer_weight, outer_bias)
    second_sum = normed.astype(jnp.float32) + outer_out
    result_f, second_pull = jax.vjp(
        layer_norm, second_sum, second_gain.astype(jnp.float32), second_bias.astype(jnp.float32)
    )
    grad_second, g_second_gain, g_second_bias = second_pull(cotangent.astype(jnp.float32))
    grad_outer = grad_second.astype(jnp.bfloat16)
    g_outer_weight = weight_grad(active, grad_outer)
    g_outer_bias = bias_grad(grad_outer)
    grad_inner = gelu_pull(back_through(grad_outer, outer_weight))[0].astype(jnp.bfloat16)
    g_inner_weight = weight_grad(normed, grad_inner)
    g_inner_bias = bias_grad(grad_inner)
    grad_normed = (back_through(grad_inner, inner_weight) + grad_second).astype(jnp.bfloat16)
    grad_first, g_first_gain, g_first_bias = first_pull(grad_normed.astype(jnp.float32))
    grad_branch = grad_first.astype(jnp.bfloat16)
    g_output_weight = weight_grad(mixture_low, grad_branch)
    g_output_bias = bias_grad(grad_branch)
    grad_mixture = back_through(grad_branch, output_weight).astype(jnp.bfloat16)
    grad_heads = grad_mixture.reshape(seq_count, row_count, HEADS, head_dim)
    row_delta = jnp.transpose(
        jnp.sum(grad_heads.astype(jnp.float32) * mixture.reshape(grad_heads.shape), axis=-1),
        (0, 2, 1),
    )
    key_all, value_all = (
        lax.all_gather(key_rows, "blk", axis=1, tiled=True),
        lax.all_gather(value_rows, "blk", axis=1, tiled=True),
    )

    def back_step(running, block_id):
        grad_query, grad_table, grad_rel_query = running
        offset = block_id * row_count
        key_block = lax.dynamic_slice_in_dim(key_all, offset, row_count, 1)
        value_block = lax.dynamic_slice_in_dim(value_all, offset, row_count, 1)
        scores, key_mask, key_heads, band_pull = block_scores(key_block, offset, True)
        value_heads = value_block.reshape(key_heads.shape)
        chances = jnp.where(key_mask, jnp.exp(scores - log_total[..., None]), 0.0)
        grad_chances = jnp.einsum(
            "sihd,sjhd->shij", grad_heads, value_heads, preferred_element_type=jnp.float32
        )
        grad_scores = (chances * (grad_chances - row_delta[..., None])).astype(jnp.bfloat16)
        grad_values = jnp.einsum(
            "shij,sihd->sjhd",
            chances.astype(jnp.bfloat16),
            grad_heads,
            preferred_element_type=jnp.float32,
        )
        grad_query = grad_query + score_scale * jnp.einsum(
            "shij,sjhd->sihd", grad_scores, key_heads, preferred_element_type=jnp.float32
        )
        grad_keys = score_scale * jnp.einsum(
            "shij,sihd->sjhd", grad_scores, query_heads, preferred_element_type=jnp.float32
        )
        grad_qtab, grad_ktab = band_pull(grad_scores.astype(jnp.float32) * score_scale)
        grad_keys = grad_keys + split_einsum("shjr,rhd->sjhd", grad_ktab, rel_queries)
        grad_rel_query = grad_rel_query + split_einsum("shjr,sjhd->rhd", grad_ktab, key_heads)
        new_state = (grad_query, grad_table + grad_qtab, grad_rel_query)
        return (
            new_state,
            (
                grad_keys.reshape(seq_count, row_count, model_width),
                grad_values.reshape(seq_count, row_count, model_width),
            ),
        )

    back_start = (
        jnp.zeros((seq_count, row_count, HEADS, head_dim), jnp.float32),
        jnp.zeros((seq_count, HEADS, row_count, rel_count), jnp.float32),
        jnp.zeros((rel_count, HEADS, head_dim), jnp.float32),
    )
    back_state, block_grads = lax.scan(back_step, back_start, block_ids)
    key_parts, value_parts = block_grads
    key_home, value_home = (
        lax.psum_scatter(
            key_parts.astype(jnp.bfloat16), "blk", scatter_dimension=0, tiled=True
        ).astype(jnp.float32),
        lax.psum_scatter(
            value_parts.astype(jnp.bfloat16), "blk", scatter_dimension=0, tiled=True
        ).astype(jnp.float32),
    )
    key_home_rows = key_home[0]
    value_home_rows = value_home[0]
    grad_query, grad_table, grad_rel_query = back_state
    grad_key_rows = key_home_rows.astype(jnp.bfloat16)
    grad_value_rows = value_home_rows.astype(jnp.bfloat16)
    grad_query = grad_query + split_einsum("shir,rhd->sihd", grad_table, rel_keys)
    grad_rel_key = split_einsum("shir,sihd->rhd", grad_table, query_heads)
    grad_query_rows = grad_query.reshape(seq_count, row_count, model_width).astype(jnp.bfloat16)
    rel_key_flat = grad_rel_key.reshape(rel_count, model_width)
    rel_query_flat = grad_rel_query.reshape(rel_count, model_width)
    g_query_weight = weight_grad(tokens, grad_query_rows) + split_einsum(
        "ro,ri->io", rel_query_flat, relative_table
    )
    g_query_bias = bias_grad(grad_query_rows) + jnp.sum(rel_query_flat, axis=0)
    g_key_weight = weight_grad(tokens, grad_key_rows) + split_einsum(
        "ro,ri->io", rel_key_flat, relative_table
    )
    g_key_bias = bias_grad(grad_key_rows) + jnp.sum(rel_key_flat, axis=0)
    g_value_weight = weight_grad(tokens, grad_value_rows)
    g_value_bias = bias_grad(grad_value_rows)
    g_relative = split_einsum("ro,io->ri", rel_query_flat, query_weight) + split_einsum(
        "ro,io->ri", rel_key_flat, key_weight
    )
    grad_tokens = (
        back_through(grad_query_rows, query_weight)
        + back_through(grad_key_rows, key_weight)
        + back_through(grad_value_rows, value_weight)
        + grad_first
    )
    (
        g_query_weight,
        g_query_bias,
        g_key_weight,
        g_key_bias,
        g_value_weight,
        g_value_bias,
        g_output_weight,
        g_output_bias,
        g_first_gain,
        g_first_bias,
        g_inner_weight,
        g_inner_bias,
        g_outer_weight,
        g_outer_bias,
        g_second_gain,
        g_second_bias,
        g_relative,
    ) = lax.psum(
        (
            g_query_weight,
            g_query_bias,
            g_key_weight,
            g_key_bias,
            g_value_weight,
            g_value_bias,
            g_output_weight,
            g_output_bias,
            g_first_gain,
            g_first_bias,
            g_inner_weight,
            g_inner_bias,
            g_outer_weight,
            g_outer_bias,
            g_second_gain,
            g_second_bias,
            g_relative,
        ),
        ("blk", "dp"),
    )
    return (
        result_f,
        grad_tokens,
        g_query_weight,
        g_query_bias,
        g_key_weight,
        g_key_bias,
        g_value_weight,
        g_value_bias,
        g_output_weight,
        g_output_bias,
        g_first_gain,
        g_first_bias,
        g_inner_weight,
        g_inner_bias,
        g_outer_weight,
        g_outer_bias,
        g_second_gain,
        g_second_bias,
        g_relative,
    )


def solution(mesh):
    in_specs = (
        P("dp", "blk", None),
        P("dp"),
        P(),
        P(),
        P(),
        P(),
        P(),
        P(),
        P(),
        P(),
        P(),
        P(),
        P(),
        P(),
        P(),
        P(),
        P(),
        P(),
        P(),
        P("dp", "blk", None),
    )
    out_specs = (
        P("dp", "blk", None),
        P("dp", "blk", None),
        P(),
        P(),
        P(),
        P(),
        P(),
        P(),
        P(),
        P(),
        P(),
        P(),
        P(),
        P(),
        P(),
        P(),
        P(),
        P(),
        P(),
    )
    return jax.shard_map(
        on_device, mesh=mesh, in_specs=in_specs, out_specs=out_specs, check_vma=False
    )
```

profile of v0, /device:TPU:0, one launch (start us, length us, event | category | flops | bytes accessed | tf_op | source)
XLA Modules:
  0.0 3081.3 jit_solution(16359634714843966742)
XLA Ops:
  64.8 37.9 %gather_fusion.3 = f32[1279,6,1024]{2,1,0:T(8,128)} fusion(f32[6,1024,512]{1,0,2:T(8,128)} %copy.85, s32[2048]{0:T(1024)S(1)} %pad_clamp_fusion.2), kind=kCustom, calls=%fused_computation.1.clone | custom fusion | bytes 62870524 | tf_op jit(solution)/shard_map/jit(_take)/gather | solution.py:34
  102.7 29.3 bitcast_select_fusion.2
  132.0 38.5 %copy.111 = f32[1,6,1024,1279]{3,2,0,1:T(8,128)} copy(f32[1,6,1024,1279]{2,1,3,0:T(8,128)} %bitcast_select_fusion.2) | data formatting | bytes 62865408
  170.4 21.6 pad.75.clone
  192.1 60.8 %reshape.862 = f32[1,6,1310720]{2,0,1:T(1,128)} reshape(f32[1,6,1024,1280]{3,2,0,1:T(8,128)} %pad.75.clone) | data formatting | bytes 62914560 | tf_op jit(solution)/shard_map/reshape | solution.py:21
  252.9 344.2 %slice_reduce_fusion.2 = f32[6,1309696]{1,0:T(8,128)} fusion(f32[1,6,1310720]{2,0,1:T(1,128)} %reshape.862), kind=kLoop, calls=%fused_computation.65 | loop fusion | bytes 62865408 | tf_op jit(solution)/shard_map/slice | solution.py:22
  597.1 597.2 %while.25 = (u32[]{:T(128)}, f32[1,6,1309696]{2,1,0:T(8,128)}, f32[7858176]{0:T(1024)}, u32[]{}, f32[]{:T(128)}, /*index=5*/u32[]{}, u32[]{}, u32[]{}) while((u32[]{:T(128)}, f32[1,6,1309696]{2,1,0:T(8,128)}, f32[7858176]{0:T(1024)}, u32[]{}, f32[]{:T(128)}, /*index=5*/u32[]{}, u32[]{}, u32[]{}) %tuple.106), condition=%wide.cond, body=%wide.body.sunk | while | flops 9 | bytes 20955336
  597.8 54.1 %dynamic-slice_reduce_fusion.2 = f32[1309696]{0:T(1024)} fusion(f32[]{:T(128)} %broadcast.449, f32[1,6,1309696]{2,1,0:T(8,128)} %get-tuple-element.749, u32[]{:T(128)S(6)} %multiply.58, u32[]{:T(128)S(6)} %multiply.59), kind=kLoop, calls=%fused_computation.219.clone.1 | loop fusion | bytes 10477580
  652.0 44.7 %dynamic-update-slice.2 = f32[7858176]{0:T(1024)} dynamic-update-slice(f32[7858176]{0:T(1024)} %get-tuple-element.742, f32[1309696]{0:T(1024)} %dynamic-slice_reduce_fusion.2, u32[]{:T(128)S(6)} %add.807) | dynamic-update-slice | bytes 10477572
  697.2 54.1 %dynamic-slice_reduce_fusion.2 = f32[1309696]{0:T(1024)} fusion(f32[]{:T(128)} %broadcast.449, f32[1,6,1309696]{2,1,0:T(8,128)} %get-tuple-element.749, u32[]{:T(128)S(6)} %multiply.58, u32[]{:T(128)S(6)} %multiply.59), kind=kLoop, calls=%fused_computation.219.clone.1 | loop fusion | bytes 10477580
  751.3 44.8 %dynamic-update-slice.2 = f32[7858176]{0:T(1024)} dynamic-update-slice(f32[7858176]{0:T(1024)} %get-tuple-element.742, f32[1309696]{0:T(1024)} %dynamic-slice_reduce_fusion.2, u32[]{:T(128)S(6)} %add.807) | dynamic-update-slice | bytes 10477572
  796.7 54.1 %dynamic-slice_reduce_fusion.2 = f32[1309696]{0:T(1024)} fusion(f32[]{:T(128)} %broadcast.449, f32[1,6,1309696]{2,1,0:T(8,128)} %get-tuple-element.749, u32[]{:T(128)S(6)} %multiply.58, u32[]{:T(128)S(6)} %multiply.59), kind=kLoop, calls=%fused_computation.219.clone.1 | loop fusion | bytes 10477580
  850.8 44.8 %dynamic-update-slice.2 = f32[7858176]{0:T(1024)} dynamic-update-slice(f32[7858176]{0:T(1024)} %get-tuple-element.742, f32[1309696]{0:T(1024)} %dynamic-slice_reduce_fusion.2, u32[]{:T(128)S(6)} %add.807) | dynamic-update-slice | bytes 10477572
  896.2 54.1 %dynamic-slice_reduce_fusion.2 = f32[1309696]{0:T(1024)} fusion(f32[]{:T(128)} %broadcast.449, f32[1,6,1309696]{2,1,0:T(8,128)} %get-tuple-element.749, u32[]{:T(128)S(6)} %multiply.58, u32[]{:T(128)S(6)} %multiply.59), kind=kLoop, calls=%fused_computation.219.clone.1 | loop fusion | bytes 10477580
  950.3 44.9 %dynamic-update-slice.2 = f32[7858176]{0:T(1024)} dynamic-update-slice(f32[7858176]{0:T(1024)} %get-tuple-element.742, f32[1309696]{0:T(1024)} %dynamic-slice_reduce_fusion.2, u32[]{:T(128)S(6)} %add.807) | dynamic-update-slice | bytes 10477572
  995.7 54.1 %dynamic-slice_reduce_fusion.2 = f32[1309696]{0:T(1024)} fusion(f32[]{:T(128)} %broadcast.449, f32[1,6,1309696]{2,1,0:T(8,128)} %get-tuple-element.749, u32[]{:T(128)S(6)} %multiply.58, u32[]{:T(128)S(6)} %multiply.59), kind=kLoop, calls=%fused_computation.219.clone.1 | loop fusion | bytes 10477580
  1049.9 44.9 %dynamic-update-slice.2 = f32[7858176]{0:T(1024)} dynamic-update-slice(f32[7858176]{0:T(1024)} %get-tuple-element.742, f32[1309696]{0:T(1024)} %dynamic-slice_reduce_fusion.2, u32[]{:T(128)S(6)} %add.807) | dynamic-update-slice | bytes 10477572
  1095.3 54.1 %dynamic-slice_reduce_fusion.2 = f32[1309696]{0:T(1024)} fusion(f32[]{:T(128)} %broadcast.449, f32[1,6,1309696]{2,1,0:T(8,128)} %get-tuple-element.749, u32[]{:T(128)S(6)} %multiply.58, u32[]{:T(128)S(6)} %multiply.59), kind=kLoop, calls=%fused_computation.219.clone.1 | loop fusion | bytes 10477580
  1149.4 44.9 %dynamic-update-slice.2 = f32[7858176]{0:T(1024)} dynamic-update-slice(f32[7858176]{0:T(1024)} %get-tuple-element.742, f32[1309696]{0:T(1024)} %dynamic-slice_reduce_fusion.2, u32[]{:T(128)S(6)} %add.807) | dynamic-update-slice | bytes 10477572
  1194.3 61.2 %reshape.993 = f32[6,1,1024,1279]{3,2,1,0:T(8,128)} reshape(f32[7858176]{0:T(1024)} %get-tuple-element.501) | data formatting | bytes 62865408
  1325.2 87.7 %slice_reduce_fusion.3 = f32[6,327424]{1,0:T(8,128)} fusion(f32[1,6,327680]{2,0,1:T(1,128)} %reshape.859), kind=kLoop, calls=%fused_computation.67 | loop fusion | bytes 15716352 | tf_op jit(solution)/shard_map/slice | solution.py:22
  1462.8 1364.8 %while.24 = (s32[]{:T(128)}, f32[1,256,6,64]{1,3,2,0:T(8,128)}, f32[1,6,256,512]{2,1,3,0:T(8,128)}, f32[512,6,64]{0,2,1:T(8,128)}, bf16[4,1,256,384]{2,3,1,0:T(8...) while((s32[]{:T(128)}, f32[1,256,6,64]{1,3,2,0:T(8,128)}, ...), condition=%wide.region_14.18_spmd.clone, body=%wide.region_11.17_spmd.clone.sunk | while | flops 768058880 | bytes 276986912 | solution.py:237
  1607.5 62.9 %scatter_fusion = f32[6,256,512]{1,0,2:T(8,128)} fusion(f32[6,256,512]{1,0,2:T(8,128)} %bitcast.495, s32[511]{0:T(512)S(1)} %compare_select_fusion.6, f32[511,6,256]{2,1,0:T(8,128)} %copy.140), kind=kCustom, calls=%fused_computation.4.clone.clone.1 | custom fusion | flops 784896 | bytes 9420796 | tf_op jit(solution)/shard_map/while/body/eval_jaxpr/transpose(jvp(jit(_take)))/scatter-add | solution.py:32
  1705.7 63.0 %scatter_fusion.1 = f32[6,256,512]{1,0,2:T(8,128)} fusion(f32[6,256,512]{1,0,2:T(8,128)} %broadcast.448, s32[511]{0:T(512)S(1)} %compare_select_fusion.7, f32[511,6,256]{2,1,0:T(8,128)} %copy.142), kind=kCustom, calls=%fused_computation.5.clone.clone.1 | custom fusion | flops 784896 | bytes 9420796 | tf_op jit(solution)/shard_map/while/body/eval_jaxpr/transpose(jvp(jit(_take)))/scatter-add | solution.py:34
  1937.9 66.6 %scatter_fusion = f32[6,256,512]{1,0,2:T(8,128)} fusion(f32[6,256,512]{1,0,2:T(8,128)} %bitcast.495, s32[511]{0:T(512)S(1)} %compare_select_fusion.6, f32[511,6,256]{2,1,0:T(8,128)} %copy.140), kind=kCustom, calls=%fused_computation.4.clone.clone.1 | custom fusion | flops 784896 | bytes 9420796 | tf_op jit(solution)/shard_map/while/body/eval_jaxpr/transpose(jvp(jit(_take)))/scatter-add | solution.py:32
  2039.7 66.7 %scatter_fusion.1 = f32[6,256,512]{1,0,2:T(8,128)} fusion(f32[6,256,512]{1,0,2:T(8,128)} %broadcast.448, s32[511]{0:T(512)S(1)} %compare_select_fusion.7, f32[511,6,256]{2,1,0:T(8,128)} %copy.142), kind=kCustom, calls=%fused_computation.5.clone.clone.1 | custom fusion | flops 784896 | bytes 9420796 | tf_op jit(solution)/shard_map/while/body/eval_jaxpr/transpose(jvp(jit(_take)))/scatter-add | solution.py:34
  2275.9 70.0 %scatter_fusion = f32[6,256,512]{1,0,2:T(8,128)} fusion(f32[6,256,512]{1,0,2:T(8,128)} %bitcast.495, s32[511]{0:T(512)S(1)} %compare_select_fusion.6, f32[511,6,256]{2,1,0:T(8,128)} %copy.140), kind=kCustom, calls=%fused_computation.4.clone.clone.1 | custom fusion | flops 784896 | bytes 9420796 | tf_op jit(solution)/shard_map/while/body/eval_jaxpr/transpose(jvp(jit(_take)))/scatter-add | solution.py:32
  2381.1 70.3 %scatter_fusion.1 = f32[6,256,512]{1,0,2:T(8,128)} fusion(f32[6,256,512]{1,0,2:T(8,128)} %broadcast.448, s32[511]{0:T(512)S(1)} %compare_select_fusion.7, f32[511,6,256]{2,1,0:T(8,128)} %copy.142), kind=kCustom, calls=%fused_computation.5.clone.clone.1 | custom fusion | flops 784896 | bytes 9420796 | tf_op jit(solution)/shard_map/while/body/eval_jaxpr/transpose(jvp(jit(_take)))/scatter-add | solution.py:34
  2620.9 70.0 %scatter_fusion = f32[6,256,512]{1,0,2:T(8,128)} fusion(f32[6,256,512]{1,0,2:T(8,128)} %bitcast.495, s32[511]{0:T(512)S(1)} %compare_select_fusion.6, f32[511,6,256]{2,1,0:T(8,128)} %copy.140), kind=kCustom, calls=%fused_computation.4.clone.clone.1 | custom fusion | flops 784896 | bytes 9420796 | tf_op jit(solution)/shard_map/while/body/eval_jaxpr/transpose(jvp(jit(_take)))/scatter-add | solution.py:32
  2726.1 70.3 %scatter_fusion.1 = f32[6,256,512]{1,0,2:T(8,128)} fusion(f32[6,256,512]{1,0,2:T(8,128)} %broadcast.448, s32[511]{0:T(512)S(1)} %compare_select_fusion.7, f32[511,6,256]{2,1,0:T(8,128)} %copy.142), kind=kCustom, calls=%fused_computation.5.clone.clone.1 | custom fusion | flops 784896 | bytes 9420796 | tf_op jit(solution)/shard_map/while/body/eval_jaxpr/transpose(jvp(jit(_take)))/scatter-add | solution.py:34
  2881.9 41.9 %all-reduce.8 = (f32[384]{0:T(512)}, f32[384]{0:T(512)}, f32[384]{0:T(512)}, f32[384]{0:T(512)}, f32[384]{0:T(512)}, /*index=5*/f32[384]{0:T(512)}, f32[1536]{0:...) all-reduce(f32[384]{0:T(512)S(1)} %add.515, ...), channel_id=1, replica_groups=mesh['blk'=4,'dp'=8] {'blk','dp'}, use_global_device_ids=true, to_apply=%region_20.24 | all-reduce | flops 4992 | bytes 39936 | tf_op jit(solution)/shard_map/psum | solution.py:294
  2925.2 138.0 %all-reduce.12.cloned.1.call-done = (f32[384,384]{0,1:T(8,128)}, f32[384,384]{0,1:T(8,128)}, f32[384,384]{0,1:T(8,128)}, f32[384,384]{1,0:T(8,128)}, f32[384,153...) async-done(((f32[384,384]{0,1:T(8,128)}, f32[384,384]{0,1:T(8,128)}, f32[384,384]{0,1:T(8,128)}, f32[384,384]{1,0:T(8,128)}, f32[384,1536]{1,0:T(8,128)}, ...) | async-done | bytes 7864336 | tf_op jit(solution)/shard_map/psum | solution.py:294
  (589 shorter events, 1058.1 us)
Async XLA Ops:
  7.2 1432.3 %copy-start = (bf16[384,1536]{1,0:T(8,128)(2,1)S(1)}, bf16[384,1536]{1,0:T(8,128)(2,1)}, u32[]{:S(2)}) copy-start(bf16[384,1536]{1,0:T(8,128)(2,1)} %param.40) | copy-start | bytes 3538948
  7.2 2851.1 %reduce-scatter.5.cloned.1.call-start = ((), (), s32[]{:S(2)}) async-start(), calls=%async_computation.3 | async-start | bytes 983040 | tf_op jit(solution)/shard_map/reduce_scatter | solution.py:243
  10.2 6.1 copy-start.82
  10.2 6.7 copy-start.83
  10.2 6.7 copy-start.42
  13.0 27.6 copy-start.6
  40.5 6.4 copy-start.18
  1261.8 7.1 copy-start.48
  1261.8 7.3 copy-start.25
  1273.7 10.2 copy-start.67
  1412.9 16.5 copy-start.19
  1437.4 7.5 copy-start.68
  1437.4 19.9 copy-start.59
  1438.8 6.1 copy-start.51
  1439.3 18.1 copy-start.13
  1439.3 18.1 copy-start.61
  1439.5 17.9 copy-start.63
  1446.9 7.6 copy-start.90
  1446.9 7.6 copy-start.91
  1463.2 7.5 copy-start.8
  1607.5 62.9 %copy-start.5 = (f32[1,6,256,256]{3,2,1,0:T(8,128)S(1)}, f32[1,6,256,256]{3,2,1,0:T(8,128)}, u32[]{:S(2)}) copy-start(f32[1,6,256,256]{3,2,1,0:T(8,128)} %get-tuple-element.726) | copy-start | bytes 4718596 | tf_op jit(solution)/shard_map/while
  1792.7 7.5 copy-start.8
  1937.9 66.6 %copy-start.5 = (f32[1,6,256,256]{3,2,1,0:T(8,128)S(1)}, f32[1,6,256,256]{3,2,1,0:T(8,128)}, u32[]{:S(2)}) copy-start(f32[1,6,256,256]{3,2,1,0:T(8,128)} %get-tuple-element.726) | copy-start | bytes 4718596 | tf_op jit(solution)/shard_map/while
  2130.7 7.5 copy-start.8
  2275.9 70.0 %copy-start.5 = (f32[1,6,256,256]{3,2,1,0:T(8,128)S(1)}, f32[1,6,256,256]{3,2,1,0:T(8,128)}, u32[]{:S(2)}) copy-start(f32[1,6,256,256]{3,2,1,0:T(8,128)} %get-tuple-element.726) | copy-start | bytes 4718596 | tf_op jit(solution)/shard_map/while
  2475.7 7.5 copy-start.8
  2620.9 70.0 %copy-start.5 = (f32[1,6,256,256]{3,2,1,0:T(8,128)S(1)}, f32[1,6,256,256]{3,2,1,0:T(8,128)}, u32[]{:S(2)}) copy-start(f32[1,6,256,256]{3,2,1,0:T(8,128)} %get-tuple-element.726) | copy-start | bytes 4718596 | tf_op jit(solution)/shard_map/while
  2827.7 50.6 %reduce-scatter.3.cloned.1.call-start = ((), (), s32[]{:S(2)}) async-start(), calls=%async_computation.2 | async-start | bytes 983040 | tf_op jit(solution)/shard_map/reduce_scatter | solution.py:240
  2828.4 234.8 %all-reduce.12.cloned.1.call-start = ((), (), s32[]{:S(2)}) async-start(), calls=%async_computation.4 | async-start | bytes 15728640 | tf_op jit(solution)/shard_map/psum | solution.py:294
  2880.4 43.8 %copy-start.29 = (f32[1,256,384]{2,1,0:T(8,128)S(1)}, f32[1,256,384]{2,1,0:T(8,128)}, u32[]{:S(2)}) copy-start(f32[1,256,384]{2,1,0:T(8,128)} %copy-done.28) | copy-start | bytes 1179652
  2880.4 43.8 %copy-start.43 = (bf16[384,384]{1,0:T(8,128)(2,1)S(1)}, bf16[384,384]{1,0:T(8,128)(2,1)}, u32[]{:S(2)}) copy-start(bf16[384,384]{1,0:T(8,128)(2,1)} %param.34) | copy-start | bytes 884740
  2880.4 43.8 %copy-start.66 = (f32[256]{0:T(256)S(1)}, f32[256]{0:T(256)}, u32[]{:S(2)}) copy-start(f32[256]{0:T(256)} %copy-done.65) | copy-start | bytes 3076
  (85 other events, 197.7 us)
Sparse Core Ops, SparseCore 0:
  2827.8 24.4 reduce-scatter.4
  2855.0 23.2 reduce-scatter.2
  2886.4 176.7 all-reduce.11
where the time goes:
time: 3120 us; the launch traced here: 3080 us
  local copies, waits for them, and re-layouts  2040 us (65%)
  other arithmetic  676 us (22%)
  waiting for transfers between devices  157 us (5%)
  matrix products  116 us (4%)
  blocking collectives  61.6 us (2%)
    unnamed x202, local copies, waits for them, and re-layouts  735 us
    slice x10, local copies, waits for them, and re-layouts, skewed(): flattened[..., row_count - 1:row_count - 1 + row_count * table_width]  523 us
    scatter-add x4, other arithmetic, band_terms(): jnp.take(key_table, key_index, axis=3)  270 us
    scatter-add x4, other arithmetic, band_terms(): jnp.take(query_table, query_index, axis=3)  269 us
    psum x1, waiting for transfers between devices, on_device(): lax.psum((g_query_weight, g_query_bias, g_key_weight, g_key_bias, g_value...  138 us
    reshape x17, local copies, waits for them, and re-layouts, skewed(): flattened.reshape(leading + (row_count, table_width))[..., :col_count]  131 us
    reshape x10, local copies, waits for them, and re-layouts, skewed(): flattened = padded.reshape(leading + (row_count * (table_width + 1),))  130 us
    pad x26, local copies, waits for them, and re-layouts, skewed(): jnp.pad(source_table, [(0, 0)] * (source_table.ndim - 1) + [(0, 1)])  120 us
  transfers between devices with their start and end apart: 3, of which 2 were waited for; matrix products, arithmetic and copies ran while one was open for 1% of the time, Pallas kernels for 0%

commit v1 on v0

--- a/solution.py
+++ b/solution.py
@@ -292,26 +292,29 @@
         g_second_bias,
         g_relative,
     ) = lax.psum(
-        (
-            g_query_weight,
-            g_query_bias,
-            g_key_weight,
-            g_key_bias,
-            g_value_weight,
-            g_value_bias,
-            g_output_weight,
-            g_output_bias,
-            g_first_gain,
-            g_first_bias,
-            g_inner_weight,
-            g_inner_bias,
-            g_outer_weight,
-            g_outer_bias,
-            g_second_gain,
-            g_second_bias,
-            g_relative,
+        lax.psum(
+            (
+                g_query_weight,
+                g_query_bias,
+                g_key_weight,
+                g_key_bias,
+                g_value_weight,
+                g_value_bias,
+                g_output_weight,
+                g_output_bias,
+                g_first_gain,
+                g_first_bias,
+                g_inner_weight,
+                g_inner_bias,
+                g_outer_weight,
+                g_outer_bias,
+                g_second_gain,
+                g_second_bias,
+                g_relative,
+            ),
+            "dp",
         ),
-        ("blk", "dp"),
+        "blk",
     )
     return (
         result_f,

time: 3120 us -> 3350 us (1.074)
  waiting for transfers between devices: 157 us -> 381 us
    psum x1, waiting for transfers between devices: 138 us -> 265 us  [on_device(): lax.psum((g_query_weight, g_query_bias, g_key_weight, g_key_bias, g_value...]
    psum x0 -> x1, waiting for transfers between devices: none -> 97.4 us  [on_device(): lax.psum(lax.psum((g_query_weight, g_query_bias, g_key_weight, g_key_bias...]
  transfers between devices with their start and end apart: 3 -> 4, of which waited for: 2 -> 3; matrix products, arithmetic and copies ran while one was open for 1% -> 1% of each run, Pallas kernels for 0% -> 0%
where the time goes in v1:
time: 3350 us; the launch traced here: 3310 us
  local copies, waits for them, and re-layouts  2040 us (61%)
  other arithmetic  676 us (20%)
  waiting for transfers between devices  381 us (11%)
  matrix products  116 us (3%)
  blocking collectives  67.7 us (2%)
    unnamed x202, local copies, waits for them, and re-layouts  735 us
    slice x10, local copies, waits for them, and re-layouts, skewed(): flattened[..., row_count - 1:row_count - 1 + row_count * table_width]  523 us
    scatter-add x4, other arithmetic, band_terms(): jnp.take(key_table, key_index, axis=3)  270 us
    scatter-add x4, other arithmetic, band_terms(): jnp.take(query_table, query_index, axis=3)  269 us
    psum x1, waiting for transfers between devices, on_device(): lax.psum((g_query_weight, g_query_bias, g_key_weight, g_key_bias, g_value...  265 us
    reshape x17, local copies, waits for them, and re-layouts, skewed(): flattened.reshape(leading + (row_count, table_width))[..., :col_count]  131 us
    reshape x10, local copies, waits for them, and re-layouts, skewed(): flattened = padded.reshape(leading + (row_count * (table_width + 1),))  130 us
    pad x26, local copies, waits for them, and re-layouts, skewed(): jnp.pad(source_table, [(0, 0)] * (source_table.ndim - 1) + [(0, 1)])  120 us
  transfers between devices with their start and end apart: 4, of which 3 were waited for; matrix products, arithmetic and copies ran while one was open for 1% of the time, Pallas kernels for 0%

profile of v1, /device:TPU:0, one launch (start us, length us, event | category | flops | bytes accessed | tf_op | source)
XLA Modules:
  0.0 3311.7 jit_solution(18417227559713901624)
XLA Ops:
  64.8 37.9 %gather_fusion.3 = f32[1279,6,1024]{2,1,0:T(8,128)} fusion(f32[6,1024,512]{1,0,2:T(8,128)} %copy.85, s32[2048]{0:T(1024)S(1)} %pad_clamp_fusion.2), kind=kCustom, calls=%fused_computation.1.clone | custom fusion | bytes 62870524 | tf_op jit(solution)/shard_map/jit(_take)/gather | solution.py:34
  102.7 29.3 bitcast_select_fusion.2
  132.0 38.5 %copy.111 = f32[1,6,1024,1279]{3,2,0,1:T(8,128)} copy(f32[1,6,1024,1279]{2,1,3,0:T(8,128)} %bitcast_select_fusion.2) | data formatting | bytes 62865408
  192.1 60.8 %reshape.862 = f32[1,6,1310720]{2,0,1:T(1,128)} reshape(f32[1,6,1024,1280]{3,2,0,1:T(8,128)} %pad.75.clone) | data formatting | bytes 62914560 | tf_op jit(solution)/shard_map/reshape | solution.py:21
  252.9 344.2 %slice_reduce_fusion.2 = f32[6,1309696]{1,0:T(8,128)} fusion(f32[1,6,1310720]{2,0,1:T(1,128)} %reshape.862), kind=kLoop, calls=%fused_computation.65 | loop fusion | bytes 62865408 | tf_op jit(solution)/shard_map/slice | solution.py:22
  597.1 597.2 %while.25 = (u32[]{:T(128)}, f32[1,6,1309696]{2,1,0:T(8,128)}, f32[7858176]{0:T(1024)}, u32[]{}, f32[]{:T(128)}, /*index=5*/u32[]{}, u32[]{}, u32[]{}) while((u32[]{:T(128)}, f32[1,6,1309696]{2,1,0:T(8,128)}, f32[7858176]{0:T(1024)}, u32[]{}, f32[]{:T(128)}, /*index=5*/u32[]{}, u32[]{}, u32[]{}) %tuple.109), condition=%wide.cond, body=%wide.body.sunk | while | flops 9 | bytes 20955336
  597.8 54.1 %dynamic-slice_reduce_fusion.2 = f32[1309696]{0:T(1024)} fusion(f32[]{:T(128)} %broadcast.449, f32[1,6,1309696]{2,1,0:T(8,128)} %get-tuple-element.766, u32[]{:T(128)S(6)} %multiply.58, u32[]{:T(128)S(6)} %multiply.59), kind=kLoop, calls=%fused_computation.219.clone.1 | loop fusion | bytes 10477580
  652.0 44.7 %dynamic-update-slice.2 = f32[7858176]{0:T(1024)} dynamic-update-slice(f32[7858176]{0:T(1024)} %get-tuple-element.759, f32[1309696]{0:T(1024)} %dynamic-slice_reduce_fusion.2, u32[]{:T(128)S(6)} %add.841) | dynamic-update-slice | bytes 10477572
  697.2 54.1 %dynamic-slice_reduce_fusion.2 = f32[1309696]{0:T(1024)} fusion(f32[]{:T(128)} %broadcast.449, f32[1,6,1309696]{2,1,0:T(8,128)} %get-tuple-element.766, u32[]{:T(128)S(6)} %multiply.58, u32[]{:T(128)S(6)} %multiply.59), kind=kLoop, calls=%fused_computation.219.clone.1 | loop fusion | bytes 10477580
  751.3 44.8 %dynamic-update-slice.2 = f32[7858176]{0:T(1024)} dynamic-update-slice(f32[7858176]{0:T(1024)} %get-tuple-element.759, f32[1309696]{0:T(1024)} %dynamic-slice_reduce_fusion.2, u32[]{:T(128)S(6)} %add.841) | dynamic-update-slice | bytes 10477572
  796.7 54.1 %dynamic-slice_reduce_fusion.2 = f32[1309696]{0:T(1024)} fusion(f32[]{:T(128)} %broadcast.449, f32[1,6,1309696]{2,1,0:T(8,128)} %get-tuple-element.766, u32[]{:T(128)S(6)} %multiply.58, u32[]{:T(128)S(6)} %multiply.59), kind=kLoop, calls=%fused_computation.219.clone.1 | loop fusion | bytes 10477580
  850.8 44.8 %dynamic-update-slice.2 = f32[7858176]{0:T(1024)} dynamic-update-slice(f32[7858176]{0:T(1024)} %get-tuple-element.759, f32[1309696]{0:T(1024)} %dynamic-slice_reduce_fusion.2, u32[]{:T(128)S(6)} %add.841) | dynamic-update-slice | bytes 10477572
  896.2 54.1 %dynamic-slice_reduce_fusion.2 = f32[1309696]{0:T(1024)} fusion(f32[]{:T(128)} %broadcast.449, f32[1,6,1309696]{2,1,0:T(8,128)} %get-tuple-element.766, u32[]{:T(128)S(6)} %multiply.58, u32[]{:T(128)S(6)} %multiply.59), kind=kLoop, calls=%fused_computation.219.clone.1 | loop fusion | bytes 10477580
  950.3 44.9 %dynamic-update-slice.2 = f32[7858176]{0:T(1024)} dynamic-update-slice(f32[7858176]{0:T(1024)} %get-tuple-element.759, f32[1309696]{0:T(1024)} %dynamic-slice_reduce_fusion.2, u32[]{:T(128)S(6)} %add.841) | dynamic-update-slice | bytes 10477572
  995.7 54.1 %dynamic-slice_reduce_fusion.2 = f32[1309696]{0:T(1024)} fusion(f32[]{:T(128)} %broadcast.449, f32[1,6,1309696]{2,1,0:T(8,128)} %get-tuple-element.766, u32[]{:T(128)S(6)} %multiply.58, u32[]{:T(128)S(6)} %multiply.59), kind=kLoop, calls=%fused_computation.219.clone.1 | loop fusion | bytes 10477580
  1049.9 44.9 %dynamic-update-slice.2 = f32[7858176]{0:T(1024)} dynamic-update-slice(f32[7858176]{0:T(1024)} %get-tuple-element.759, f32[1309696]{0:T(1024)} %dynamic-slice_reduce_fusion.2, u32[]{:T(128)S(6)} %add.841) | dynamic-update-slice | bytes 10477572
  1095.3 54.1 %dynamic-slice_reduce_fusion.2 = f32[1309696]{0:T(1024)} fusion(f32[]{:T(128)} %broadcast.449, f32[1,6,1309696]{2,1,0:T(8,128)} %get-tuple-element.766, u32[]{:T(128)S(6)} %multiply.58, u32[]{:T(128)S(6)} %multiply.59), kind=kLoop, calls=%fused_computation.219.clone.1 | loop fusion | bytes 10477580
  1149.4 44.9 %dynamic-update-slice.2 = f32[7858176]{0:T(1024)} dynamic-update-slice(f32[7858176]{0:T(1024)} %get-tuple-element.759, f32[1309696]{0:T(1024)} %dynamic-slice_reduce_fusion.2, u32[]{:T(128)S(6)} %add.841) | dynamic-update-slice | bytes 10477572
  1194.3 61.2 %reshape.993 = f32[6,1,1024,1279]{3,2,1,0:T(8,128)} reshape(f32[7858176]{0:T(1024)} %get-tuple-element.501) | data formatting | bytes 62865408
  1325.2 87.7 %slice_reduce_fusion.3 = f32[6,327424]{1,0:T(8,128)} fusion(f32[1,6,327680]{2,0,1:T(1,128)} %reshape.859), kind=kLoop, calls=%fused_computation.67 | loop fusion | bytes 15716352 | tf_op jit(solution)/shard_map/slice | solution.py:22
  1462.8 1364.8 %while.24 = (s32[]{:T(128)}, f32[1,256,6,64]{1,3,2,0:T(8,128)}, f32[1,6,256,512]{2,1,3,0:T(8,128)}, f32[512,6,64]{0,2,1:T(8,128)}, bf16[4,1,256,384]{2,3,1,0:T(8...) while((s32[]{:T(128)}, f32[1,256,6,64]{1,3,2,0:T(8,128)}, ...), condition=%wide.region_14.18_spmd.clone, body=%wide.region_11.17_spmd.clone.sunk | while | flops 768058880 | bytes 276986912 | solution.py:237
  1607.5 62.9 %scatter_fusion = f32[6,256,512]{1,0,2:T(8,128)} fusion(f32[6,256,512]{1,0,2:T(8,128)} %bitcast.495, s32[511]{0:T(512)S(1)} %compare_select_fusion.6, f32[511,6,256]{2,1,0:T(8,128)} %copy.140), kind=kCustom, calls=%fused_computation.4.clone.clone.1 | custom fusion | flops 784896 | bytes 9420796 | tf_op jit(solution)/shard_map/while/body/eval_jaxpr/transpose(jvp(jit(_take)))/scatter-add | solution.py:32
  1705.6 63.0 %scatter_fusion.1 = f32[6,256,512]{1,0,2:T(8,128)} fusion(f32[6,256,512]{1,0,2:T(8,128)} %broadcast.448, s32[511]{0:T(512)S(1)} %compare_select_fusion.7, f32[511,6,256]{2,1,0:T(8,128)} %copy.142), kind=kCustom, calls=%fused_computation.5.clone.clone.1 | custom fusion | flops 784896 | bytes 9420796 | tf_op jit(solution)/shard_map/while/body/eval_jaxpr/transpose(jvp(jit(_take)))/scatter-add | solution.py:34
  1937.9 66.6 %scatter_fusion = f32[6,256,512]{1,0,2:T(8,128)} fusion(f32[6,256,512]{1,0,2:T(8,128)} %bitcast.495, s32[511]{0:T(512)S(1)} %compare_select_fusion.6, f32[511,6,256]{2,1,0:T(8,128)} %copy.140), kind=kCustom, calls=%fused_computation.4.clone.clone.1 | custom fusion | flops 784896 | bytes 9420796 | tf_op jit(solution)/shard_map/while/body/eval_jaxpr/transpose(jvp(jit(_take)))/scatter-add | solution.py:32
  2039.7 66.7 %scatter_fusion.1 = f32[6,256,512]{1,0,2:T(8,128)} fusion(f32[6,256,512]{1,0,2:T(8,128)} %broadcast.448, s32[511]{0:T(512)S(1)} %compare_select_fusion.7, f32[511,6,256]{2,1,0:T(8,128)} %copy.142), kind=kCustom, calls=%fused_computation.5.clone.clone.1 | custom fusion | flops 784896 | bytes 9420796 | tf_op jit(solution)/shard_map/while/body/eval_jaxpr/transpose(jvp(jit(_take)))/scatter-add | solution.py:34
  2275.9 70.0 %scatter_fusion = f32[6,256,512]{1,0,2:T(8,128)} fusion(f32[6,256,512]{1,0,2:T(8,128)} %bitcast.495, s32[511]{0:T(512)S(1)} %compare_select_fusion.6, f32[511,6,256]{2,1,0:T(8,128)} %copy.140), kind=kCustom, calls=%fused_computation.4.clone.clone.1 | custom fusion | flops 784896 | bytes 9420796 | tf_op jit(solution)/shard_map/while/body/eval_jaxpr/transpose(jvp(jit(_take)))/scatter-add | solution.py:32
  2381.1 70.3 %scatter_fusion.1 = f32[6,256,512]{1,0,2:T(8,128)} fusion(f32[6,256,512]{1,0,2:T(8,128)} %broadcast.448, s32[511]{0:T(512)S(1)} %compare_select_fusion.7, f32[511,6,256]{2,1,0:T(8,128)} %copy.142), kind=kCustom, calls=%fused_computation.5.clone.clone.1 | custom fusion | flops 784896 | bytes 9420796 | tf_op jit(solution)/shard_map/while/body/eval_jaxpr/transpose(jvp(jit(_take)))/scatter-add | solution.py:34
  2620.9 70.0 %scatter_fusion = f32[6,256,512]{1,0,2:T(8,128)} fusion(f32[6,256,512]{1,0,2:T(8,128)} %bitcast.495, s32[511]{0:T(512)S(1)} %compare_select_fusion.6, f32[511,6,256]{2,1,0:T(8,128)} %copy.140), kind=kCustom, calls=%fused_computation.4.clone.clone.1 | custom fusion | flops 784896 | bytes 9420796 | tf_op jit(solution)/shard_map/while/body/eval_jaxpr/transpose(jvp(jit(_take)))/scatter-add | solution.py:32
  2726.1 70.3 %scatter_fusion.1 = f32[6,256,512]{1,0,2:T(8,128)} fusion(f32[6,256,512]{1,0,2:T(8,128)} %broadcast.448, s32[511]{0:T(512)S(1)} %compare_select_fusion.7, f32[511,6,256]{2,1,0:T(8,128)} %copy.142), kind=kCustom, calls=%fused_computation.5.clone.clone.1 | custom fusion | flops 784896 | bytes 9420796 | tf_op jit(solution)/shard_map/while/body/eval_jaxpr/transpose(jvp(jit(_take)))/scatter-add | solution.py:34
  2880.3 264.8 %all-reduce.15.cloned.1.call-done = (f32[384,384]{0,1:T(8,128)}, f32[384,384]{0,1:T(8,128)}, f32[384,384]{0,1:T(8,128)}, f32[384,384]{1,0:T(8,128)}, f32[384,153...) async-done(((f32[384,384]{0,1:T(8,128)}, f32[384,384]{0,1:T(8,128)}, f32[384,384]{0,1:T(8,128)}, f32[384,384]{1,0:T(8,128)}, f32[384,1536]{1,0:T(8,128)}, ...) | async-done | bytes 7864336 | tf_op jit(solution)/shard_map/psum | solution.py:295
  3146.7 35.1 %all-reduce.8 = (f32[384]{0:T(512)S(1)}, f32[384]{0:T(512)S(1)}, f32[384]{0:T(512)S(1)}, f32[384]{0:T(512)S(1)}, f32[384]{0:T(512)S(1)}, /*index=5*/f32[384]{0:T...) all-reduce(f32[384]{0:T(512)S(1)} %add.549, ...), channel_id=1, replica_groups=mesh['blk'=4,'dp'=8] {'dp'}, use_global_device_ids=true, to_apply=%region_21.25 | all-reduce | flops 4992 | bytes 39936 | tf_op jit(solution)/shard_map/psum | solution.py:295
  3196.2 97.4 %all-reduce.17.cloned.1.call-done = (f32[384,384]{0,1:T(8,128)}, f32[384,384]{0,1:T(8,128)}, f32[384,384]{0,1:T(8,128)}, f32[384,384]{1,0:T(8,128)}, f32[384,153...) async-done(((f32[384,384]{0,1:T(8,128)}, f32[384,384]{0,1:T(8,128)}, f32[384,384]{0,1:T(8,128)}, f32[384,384]{1,0:T(8,128)}, f32[384,1536]{1,0:T(8,128)}, ...) | async-done | bytes 7864336 | tf_op jit(solution)/shard_map/psum | solution.py:294
  (593 shorter events, 1092.6 us)
Async XLA Ops:
  7.2 1432.3 %copy-start = (bf16[384,1536]{1,0:T(8,128)(2,1)S(1)}, bf16[384,1536]{1,0:T(8,128)(2,1)}, u32[]{:S(2)}) copy-start(bf16[384,1536]{1,0:T(8,128)(2,1)} %param.40) | copy-start | bytes 3538948
  7.2 2851.1 %reduce-scatter.5.cloned.1.call-start = ((), (), s32[]{:S(2)}) async-start(), calls=%async_computation.3 | async-start | bytes 983040 | tf_op jit(solution)/shard_map/reduce_scatter | solution.py:243
  10.2 6.1 copy-start.82
  10.2 6.7 copy-start.83
  10.2 6.7 copy-start.42
  13.0 27.6 copy-start.6
  40.5 6.4 copy-start.18
  1261.8 7.1 copy-start.48
  1261.8 7.3 copy-start.25
  1273.7 10.2 copy-start.67
  1412.9 16.5 copy-start.19
  1437.4 7.5 copy-start.68
  1437.4 19.9 copy-start.59
  1439.3 18.1 copy-start.13
  1439.3 18.1 copy-start.61
  1439.5 17.9 copy-start.63
  1446.9 7.6 copy-start.90
  1446.9 7.6 copy-start.91
  1463.2 7.5 copy-start.8
  1607.5 62.9 %copy-start.5 = (f32[1,6,256,256]{3,2,1,0:T(8,128)S(1)}, f32[1,6,256,256]{3,2,1,0:T(8,128)}, u32[]{:S(2)}) copy-start(f32[1,6,256,256]{3,2,1,0:T(8,128)} %get-tuple-element.743) | copy-start | bytes 4718596 | tf_op jit(solution)/shard_map/while
  1792.7 7.5 copy-start.8
  1937.9 66.6 %copy-start.5 = (f32[1,6,256,256]{3,2,1,0:T(8,128)S(1)}, f32[1,6,256,256]{3,2,1,0:T(8,128)}, u32[]{:S(2)}) copy-start(f32[1,6,256,256]{3,2,1,0:T(8,128)} %get-tuple-element.743) | copy-start | bytes 4718596 | tf_op jit(solution)/shard_map/while
  2130.6 7.5 copy-start.8
  2275.9 70.0 %copy-start.5 = (f32[1,6,256,256]{3,2,1,0:T(8,128)S(1)}, f32[1,6,256,256]{3,2,1,0:T(8,128)}, u32[]{:S(2)}) copy-start(f32[1,6,256,256]{3,2,1,0:T(8,128)} %get-tuple-element.743) | copy-start | bytes 4718596 | tf_op jit(solution)/shard_map/while
  2475.6 7.5 copy-start.8
  2620.9 70.0 %copy-start.5 = (f32[1,6,256,256]{3,2,1,0:T(8,128)S(1)}, f32[1,6,256,256]{3,2,1,0:T(8,128)}, u32[]{:S(2)}) copy-start(f32[1,6,256,256]{3,2,1,0:T(8,128)} %get-tuple-element.743) | copy-start | bytes 4718596 | tf_op jit(solution)/shard_map/while
  2827.6 50.6 %reduce-scatter.3.cloned.1.call-start = ((), (), s32[]{:S(2)}) async-start(), calls=%async_computation.2 | async-start | bytes 983040 | tf_op jit(solution)/shard_map/reduce_scatter | solution.py:240
  2828.4 316.7 %all-reduce.15.cloned.1.call-start = ((), (), s32[]{:S(2)}) async-start(), calls=%async_computation.4 | async-start | bytes 15728640 | tf_op jit(solution)/shard_map/psum | solution.py:295
  2880.3 413.3 %all-reduce.17.cloned.1.call-start = ((), (), s32[]{:S(2)}) async-start(), calls=%async_computation.5 | async-start | bytes 15728640 | tf_op jit(solution)/shard_map/psum | solution.py:294
  3145.2 49.9 %copy-start.29 = (f32[1,256,384]{2,1,0:T(8,128)S(1)}, f32[1,256,384]{2,1,0:T(8,128)}, u32[]{:S(2)}) copy-start(f32[1,256,384]{2,1,0:T(8,128)} %copy-done.28) | copy-start | bytes 1179652
  3145.2 49.9 %copy-start.43 = (bf16[384,384]{1,0:T(8,128)(2,1)S(1)}, bf16[384,384]{1,0:T(8,128)(2,1)}, u32[]{:S(2)}) copy-start(bf16[384,384]{1,0:T(8,128)(2,1)} %param.34) | copy-start | bytes 884740
  3145.2 49.9 %copy-start.66 = (f32[256]{0:T(256)S(1)}, f32[256]{0:T(256)}, u32[]{:S(2)}) copy-start(f32[256]{0:T(256)} %copy-done.65) | copy-start | bytes 3076
  (86 other events, 203.7 us)
Sparse Core Ops, SparseCore 0:
  2827.7 24.4 reduce-scatter.4
  2854.9 23.2 reduce-scatter.2
  2885.4 259.6 all-reduce.14
  3147.8 145.7 all-reduce.16
